TPU v7x, 128 devices: a whole 4x4x4 slice. The times are simulated.
128 devices in a mesh: tm: 16 (over x, y_hi, core), freq: 8 (over z, y_lo).
Axes of the slice: x: 4, y: 4 (y_hi: 2, y_lo: 2; y = y_hi * 2 + y_lo), z: 4, core: 2. Of those that a mesh axis runs over, the one named last changes fastest.
Arguments:
- visibilities: bfloat16 [2, 128, 768, 4096], P(None, None, 'freq', 'tm'), may hold values from -6 to 6
- counts: int32 [128], replicated, may hold values from 1 to 255
- beam_inverse: bfloat16 [64, 768, 2, 64, 128], P('tm', 'freq'), may hold values from -0.375 to 0.375
- kl_modes: bfloat16 [64, 128, 768], P('tm'), may hold values from -0.21875 to 0.21875
Outputs:
- filtered: bfloat16 [64, 64, 2, 128], P('freq', 'tm')
All inputs are finite; a program needn't handle non-finite values.
Results may differ from a plain program's by a relative error of at most 0.0085.
Values may be sent and summed in bfloat16 or wider, within the bound.
A program may use at most 128 MiB of HBM per device.

v0:
```python
import math

import jax
import jax.numpy as jnp
from jax import lax
from jax.sharding import PartitionSpec as P


def dft_table(modes, times, total):
    phase = modes[:, None] * times[None, :] % total
    angle = phase.astype(jnp.float32) * (2.0 * math.pi / total)
    cosine = jnp.cos(angle)
    sine = jnp.sin(angle)
    table = jnp.stack([jnp.stack([cosine, sine], 1), jnp.stack([-sine, cosine], 1)], 1)
    return table.astype(jnp.bfloat16)


def local(visibilities, counts, beam_inverse, kl_modes):
    stacks = visibilities.shape[1]
    time_rows = visibilities.shape[3]
    time_group = lax.axis_size("tm")
    total_time = time_rows * time_group
    mode_rows = beam_inverse.shape[0]
    all_modes = mode_rows * time_group
    weights = jnp.sqrt(counts.astype(jnp.float32)) * (1.0 / math.sqrt(128.0 * total_time))
    stack_rows = stacks // time_group
    local_weights = lax.dynamic_slice_in_dim(weights, lax.axis_index("tm") * stack_rows, stack_rows)
    table = dft_table(
        jnp.arange(all_modes, dtype=jnp.int32), jnp.arange(total_time, dtype=jnp.int32), total_time
    )
    summed = jnp.einsum(
        "mqpt,pbft->mqbf",
        table,
        lax.all_to_all(visibilities, "tm", split_axis=1, concat_axis=3, tiled=True),
        preferred_element_type=jnp.float32,
    )
    local_modes = (summed * local_weights[None, None, :, None]).astype(jnp.bfloat16)
    spectrum = lax.all_to_all(local_modes, "tm", split_axis=0, concat_axis=2, tiled=True)
    terms = jnp.einsum(
        "mfplb,mqbf->mpqlf", beam_inverse, spectrum, preferred_element_type=jnp.float32
    )
    sky = jnp.stack([terms[:, 0, 0] - terms[:, 1, 1], terms[:, 0, 1] + terms[:, 1, 0]], 1).astype(
        jnp.bfloat16
    )
    full_bands = lax.all_to_all(sky, "freq", split_axis=2, concat_axis=3, tiled=True)
    filtered = jnp.einsum(
        "mkf,mqlf->lmqk", kl_modes, full_bands, preferred_element_type=jnp.float32
    )
    return filtered.astype(jnp.bfloat16)


def solution(mesh):
    in_specs = (
        P(None, None, "freq", "tm"),
        P(),
        P("tm", "freq", None, None, None),
        P("tm", None, None),
    )
    out_specs = P("freq", "tm", None, None)
    return jax.shard_map(local, mesh=mesh, in_specs=in_specs, out_specs=out_specs, check_vma=False)
```

profile of v0, /device:TPU:0, one launch (start us, length us, event | category | flops | bytes accessed | tf_op | source)
XLA Modules:
  0.0 305.8 jit_solution(8103130283848185372)
XLA Ops:
  0.0 0.0 copy-start
  0.0 10.9 %copy.38 = bf16[2,128,96,256]{3,2,0,1:T(8,128)(2,1)} copy(bf16[2,128,96,256]{3,2,1,0:T(8,128)(2,1)} %param.4) | data formatting | bytes 25165824 | tf_op args[0]
  10.9 0.0 copy-start.1
  10.9 7.3 %all-to-all-start = ((bf16[2,128,96,256]{3,2,0,1:T(8,128)(2,1)}), bf16[2,128,96,256]{3,2,0,1:T(8,128)(2,1)}, u32[]{:S(2)}, u32[]{:S(2)}) async-start(bf16[2,128,96,256]{3,2,0,1:T(8,128)(2,1)} %copy.38), calls=%async_computation | async-start | bytes 25165824 | tf_op jit(solution)/shard_map/all_to_all | solution.py:34
  18.3 0.0 copy-done.1
  18.3 0.1 dynamic_slice.3
  18.4 3.9 %fusion.15 = bf16[64,1,4096]{2,0,1:T(8,128)(2,1)S(1)} fusion(), kind=kLoop, calls=%fused_computation.25 | loop fusion | flops 3932160 | bytes 524288 | tf_op jit(solution)/shard_map/convert.11
  22.3 4.3 %negate_convert_fusion = (bf16[64,1,4096]{2,0,1:T(8,128)(2,1)S(1)}, bf16[64,1,4096]{2,0,1:T(8,128)(2,1)S(1)}) fusion(), kind=kLoop, calls=%fused_computation.18 | loop fusion | flops 4456448 | bytes 1048576 | tf_op jit(solution)/shard_map/convert.7
  26.6 0.2 maximum_bitcast_fusion.8
  26.8 192.1 %all-to-all-done = bf16[2,128,96,256]{3,2,0,1:T(8,128)(2,1)} async-done(((bf16[2,128,96,256]{3,2,0,1:T(8,128)(2,1)}), bf16[2,128,96,256]{3,2,0,1:T(8,128)(2,1)}, u32[]{:S(2)}, u32[]{:S(2)}) %all-to-all-start) | async-done | bytes 12582944 | tf_op jit(solution)/shard_map/all_to_all | solution.py:34
  218.9 14.1 %copy.57 = bf16[2,16,8,96,256]{4,1,3,0,2:T(8,128)(2,1)} copy(bf16[2,16,8,96,256]{4,3,0,2,1:T(8,128)(2,1)} %bitcast.4) | data formatting | bytes 25165824 | tf_op jit(solution)/shard_map/all_to_all | solution.py:34
  233.0 19.5 %reshape.115 = bf16[2,8,96,4096,1]{3,2,0,1,4:T(8,128)(2,1)} reshape(bf16[2,8,96,16,256]{4,3,2,0,1:T(8,128)(2,1)} %bitcast.61) | data formatting | bytes 25165824 | tf_op jit(solution)/shard_map/all_to_all | solution.py:34
  252.5 8.2 %fusion.5 = bf16[64,2,8,96]{3,0,2,1:T(8,128)(2,1)S(1)} fusion(bf16[2,8,96,4096,1]{3,2,0,1,4:T(8,128)(2,1)} %reshape.115, bf16[64,1,2,4096]{3,0,2,1:T(8,128)(2,1)S(1)} %get-tuple-element.8, bf16[64,1,2,4096]{3,0,2,1:T(8,128)(2,1)S(1)} %get-tuple-element.7, f32[8]{0:T(128)S(1)} %dynamic_slice.3), kind=kOutput, calls=%fused_computation.10 | convolution fusion | flops 1615003648 | bytes 14876704 | tf_op jit(solution)/shard_map/mqpt,pbft->mqbf/dot_general | solution.py:31
  260.7 0.2 copy.40
  260.9 16.7 %all_to_all.54 = bf16[64,2,8,96]{3,2,1,0:T(8,128)(2,1)S(1)} all-to-all(bf16[64,2,8,96]{3,2,1,0:T(8,128)(2,1)S(1)} %copy.40), channel_id=1, replica_groups=mesh['tm'=16,'freq'=8] {'tm'}, dimensions={0} | all-to-all | bytes 393216 | tf_op jit(solution)/shard_map/all_to_all | solution.py:38
  277.6 0.2 copy.50
  277.8 14.4 %fusion.21 = f32[4,96,2,2,64]{4,2,3,1,0:T(2,128)S(1)} fusion(bf16[4,2,128,96,1]{2,1,4,3,0:T(2,128)(2,1)S(1)} %copy.50, bf16[4,96,2,64,128]{4,3,2,1,0:T(8,128)(2,1)} %param.6), kind=kOutput, calls=%fused_computation.37 | convolution fusion | flops 25165824 | bytes 13172736 | tf_op jit(solution)/shard_map/mfplb,mqbf->mpqlf/dot_general | solution.py:39
  292.1 0.4 copy.43
  292.6 0.1 copy.44
  292.7 11.9 %all_to_all.55 = bf16[4,2,64,96]{3,0,1,2:T(4,128)(2,1)S(1)} all-to-all(bf16[4,2,64,96]{3,0,1,2:T(4,128)(2,1)S(1)} %copy.44), channel_id=1, replica_groups=mesh['tm'=16,'freq'=8] {'freq'}, dimensions={2} | all-to-all | bytes 196608 | tf_op jit(solution)/shard_map/all_to_all | solution.py:45
  304.7 0.1 all_to_all.50
  304.9 0.0 copy-done
  304.9 0.3 fusion.6
  305.2 0.6 copy.47
  (6 shorter events, 0.2 us)
Async XLA Ops:
  0.0 304.9 %copy-start = (bf16[4,128,768]{2,1,0:T(8,128)(2,1)S(1)}, bf16[4,128,768]{2,1,0:T(8,128)(2,1)}, u32[]{:S(2)}) copy-start(bf16[4,128,768]{2,1,0:T(8,128)(2,1)} %param.7) | copy-start | bytes 2359300
  10.9 7.3 %copy-start.1 = (s32[128]{0:T(128)S(1)}, s32[128]{0:T(128)}, u32[]{:S(2)}) copy-start(s32[128]{0:T(128)} %param.5) | copy-start | bytes 1540
  10.9 207.9 %all-to-all-start = ((bf16[2,128,96,256]{3,2,0,1:T(8,128)(2,1)}), bf16[2,128,96,256]{3,2,0,1:T(8,128)(2,1)}, u32[]{:S(2)}, u32[]{:S(2)}) async-start(bf16[2,128,96,256]{3,2,0,1:T(8,128)(2,1)} %copy.38), calls=%async_computation | async-start | bytes 25165824 | tf_op jit(solution)/shard_map/all_to_all | solution.py:34
where the time goes:
time: 307 us; the launch traced here: 306 us
  waiting for transfers between devices  192 us (63%)
  local copies, waits for them, and re-layouts  46.4 us (15%)
  blocking collectives  28.6 us (9%)
  matrix products  22.8 us (7%)
  other arithmetic  8.51 us (3%)
  starting transfers between devices  7.29 us (2%)
    all_to_all x1, waiting for transfers between devices, local(): lax.all_to_all(visibilities, 'tm', split_axis=1, concat_axis=3, tiled=True)  192 us
    all_to_all x2, local copies, waits for them, and re-layouts, local(): lax.all_to_all(visibilities, 'tm', split_axis=1, concat_axis=3, tiled=True)  33.6 us
    all_to_all x1, blocking collectives, local(): lax.all_to_all(local_modes, 'tm', split_axis=0, concat_axis=2, tiled=True)  16.7 us
    dot_general x1, matrix products, local(): jnp.einsum('mfplb,mqbf->mpqlf', beam_inverse, spectrum, preferred_element...  14.4 us
    all_to_all x1, blocking collectives, local(): lax.all_to_all(sky, 'freq', split_axis=2, concat_axis=3, tiled=True)  11.9 us
    unnamed x5, local copies, waits for them, and re-layouts  10.9 us
    another operation x2, other arithmetic  8.25 us
    dot_general x1, matrix products, local(): jnp.einsum('mqpt,pbft->mqbf', table, lax.all_to_all(visibilities, 'tm', s...  8.16 us
  transfers between devices with their start and end apart: 1, of which 1 were waited for; matrix products, arithmetic and copies ran while one was open for 3% of the time, Pallas kernels for 0%

commit v1 on v0

v1 whole, which is shorter than its diff:
```python
import functools
import math

import jax
import jax.numpy as jnp
import ml_dtypes
import numpy as np
from jax import lax
from jax.experimental import pallas as pl
from jax.experimental.pallas import tpu as pltpu
from jax.sharding import PartitionSpec as P

RANK = 12
STRONG = (2, 3, 4, 5)
ROWS = 2 * RANK + 2 * len(STRONG)
F32 = jnp.float32
BF16 = jnp.bfloat16


def window_factors(modes, window, windows):
    total = window * windows
    step = 2.0 * math.pi / total
    m = np.arange(modes, dtype=np.float64)
    t = np.arange(window, dtype=np.float64)
    mc, tc = (modes - 1) / 2.0, (window - 1) / 2.0
    diag = -np.cos(math.pi * (2 * t + 1 - window) / total) * math.cos(math.pi * modes / total)
    off = np.sin(math.pi * (t[:-1] + 1) / total) * np.sin(math.pi * (window - 1 - t[:-1]) / total)
    _, vectors = np.linalg.eigh(np.diag(diag) + np.diag(off, 1) + np.diag(off, -1))
    return m, t, mc, tc, step, vectors


def prolate(modes, window, windows):
    m, t, mc, tc, step, vectors = window_factors(modes, window, windows)
    centred = np.exp(-1j * step * np.outer(m - mc, t - tc))
    strength = np.linalg.norm(centred @ vectors, axis=0)
    basis = vectors[:, np.argsort(-strength)[:RANK]].T
    basis = basis * np.sign(basis[:, :window // 3].sum(1))[:, None]
    expand = centred @ basis.T
    project = basis * np.exp(-1j * step * mc * (t - tc))[None]
    return m, tc, step, expand, project


def halves(x):
    x = np.round(x * 2.0**22) / 2.0**22
    high = x.astype(np.float32).astype(ml_dtypes.bfloat16)
    low = (x - high.astype(np.float64)).astype(np.float32).astype(ml_dtypes.bfloat16)
    return np.concatenate([high, low], 0)


def factors(modes, window, windows):
    m, tc, step, expand, project = prolate(modes, window, windows)
    order = list(STRONG) + [k for k in range(RANK) if k not in STRONG]
    lead = len(STRONG)
    rows = [(k, part) for part in (0, 1) for k in order[:lead]]
    rows += [(k, part) for part in (0, 1) for k in order[lead:]]
    g = np.zeros((2 * RANK, 2, window))
    for at, (k, part) in enumerate(rows):
        re, im = project[k].real, project[k].imag
        g[at] = (re, -im) if part == 0 else (im, re)
    e = np.zeros((modes, 2, windows, ROWS))
    for w in range(windows):
        turned = expand * np.exp(-1j * step * m * (w * window + tc))[:, None]
        for at, (k, part) in enumerate(rows):
            re, im = turned[:, k].real, turned[:, k].imag
            e[:, 0, w, at] = re if part == 0 else -im
            e[:, 1, w, at] = im if part == 0 else re
    e[..., 2 * RANK:] = e[..., :2 * lead]
    return halves(g.reshape(2 * RANK, 2 * window)), halves(e.reshape(2 * modes, windows * ROWS))


def kernel(
    counts, vis, beam, kl, g, e, out,
    visb, beamb, klb, klp, gb, eb, ysend, yrecv, ssend, srecv, wf, wmat, skysend, skyrecv,
    vis_sem, beam_sem, misc_sem, ys_sem, yr_sem, ss_sem, sr_sem, ks_sem, kr_sem,
    *, tm, nf, total,
):
    me = lax.axis_index("tm")
    mf = lax.axis_index("freq")
    lanes = visb.shape[2]
    half = lanes // 2
    modes = beamb.shape[0]
    band = beamb.shape[1]
    window = visb.shape[3]

    g_copy = pltpu.make_async_copy(g, gb, misc_sem.at[0])
    e_copy = pltpu.make_async_copy(e, eb, misc_sem.at[1])
    kl_copy = pltpu.make_async_copy(kl, klb, misc_sem.at[2])
    g_copy.start()

    def vis_copy(j):
        return pltpu.make_async_copy(vis.at[:, j], visb.at[j], vis_sem.at[j])

    def beam_copy(m):
        return pltpu.make_async_copy(beam.at[m], beamb.at[m], beam_sem.at[m])

    def start_vis(d, c):
        vis_copy(lax.rem(me + d, tm)).start()
        return c

    lax.fori_loop(1, tm + 1, start_vis, 0)
    e_copy.start()
    kl_copy.start()
    for m in range(modes):
        beam_copy(m).start()

    barrier = pltpu.get_barrier_semaphore()

    def greet_tm(d, c):
        pl.semaphore_signal(barrier, inc=1, device_id={"tm": lax.rem(me + d, tm)}, device_id_type=pl.DeviceIdType.MESH)
        return c

    def greet_f(d, c):
        pl.semaphore_signal(barrier, inc=1, device_id={"freq": lax.rem(mf + d, nf)}, device_id_type=pl.DeviceIdType.MESH)
        return c

    lax.fori_loop(1, tm, greet_tm, 0)
    lax.fori_loop(1, nf, greet_f, 0)
    pl.semaphore_wait(barrier, tm + nf - 2)

    def y_copy(j):
        return pltpu.make_async_remote_copy(
            src_ref=ysend.at[j], dst_ref=yrecv.at[me], send_sem=ys_sem.at[j], recv_sem=yr_sem.at[me],
            device_id={"tm": j}, device_id_type=pl.DeviceIdType.MESH)

    def y_from(s):
        return pltpu.make_async_remote_copy(
            src_ref=ysend.at[s], dst_ref=yrecv.at[s], send_sem=ys_sem.at[s], recv_sem=yr_sem.at[s],
            device_id={"tm": s}, device_id_type=pl.DeviceIdType.MESH)

    def s_copy(j):
        return pltpu.make_async_remote_copy(
            src_ref=ssend.at[j], dst_ref=srecv.at[me], send_sem=ss_sem.at[j], recv_sem=sr_sem.at[me],
            device_id={"tm": j}, device_id_type=pl.DeviceIdType.MESH)

    def s_from(s):
        return pltpu.make_async_remote_copy(
            src_ref=ssend.at[s], dst_ref=srecv.at[s], send_sem=ss_sem.at[s], recv_sem=sr_sem.at[s],
            device_id={"tm": s}, device_id_type=pl.DeviceIdType.MESH)

    def k_copy(m, j):
        return pltpu.make_async_remote_copy(
            src_ref=skysend.at[m, j], dst_ref=skyrecv.at[m, mf], send_sem=ks_sem.at[m, j], recv_sem=kr_sem.at[m, mf],
            device_id={"freq": j}, device_id_type=pl.DeviceIdType.MESH)

    def k_from(m, s):
        return pltpu.make_async_remote_copy(
            src_ref=skysend.at[m, s], dst_ref=skyrecv.at[m, s], send_sem=ks_sem.at[m, s], recv_sem=kr_sem.at[m, s],
            device_id={"freq": s}, device_id_type=pl.DeviceIdType.MESH)

    g_copy.wait()
    nt = (((1,), (1,)), ((), ()))

    def project(j):
        vis_copy(j).wait()
        y2 = lax.dot_general(gb[:, :window], visb[j, 0], nt, preferred_element_type=F32)
        y2 = y2 + lax.dot_general(gb[:, window:], visb[j, 1], nt, preferred_element_type=F32)
        y = y2[:2 * RANK] + y2[2 * RANK:]
        strong = y[:2 * len(STRONG)]
        low = strong - strong.astype(BF16).astype(F32)
        return jnp.concatenate([y, low], 0).astype(BF16)

    def send_y(d, c):
        j = lax.rem(me + d, tm)
        ysend[j] = project(j)
        y_copy(j).start()
        return c

    lax.fori_loop(1, tm, send_y, 0)
    yrecv[me] = project(me)

    kl_copy.wait()

    def spread(m, c):
        zero = jnp.zeros((klb.shape[1], 128 - band), BF16)
        for s in range(nf):
            klp[m, :, s * 128:(s + 1) * 128] = jnp.concatenate([klb[m, :, s * band:(s + 1) * band], zero], 1)
        return c

    lax.fori_loop(0, modes, spread, 0)

    lane = lax.broadcasted_iota(jnp.int32, (1, lanes), 1) // band
    share = lanes // band
    count = jnp.zeros((1, lanes), F32)
    for i in range(share):
        count = jnp.where(lane == i, counts[me * share + i].astype(F32), count)
    factor = jnp.sqrt(count) * (1.0 / math.sqrt(128.0 * total))

    e_copy.wait()

    def wait_y(d, c):
        y_from(lax.rem(me + tm - d, tm)).wait_recv()
        return c

    lax.fori_loop(1, tm, wait_y, 0)
    parts = []
    for h in range(2):
        y = yrecv[:, :, h * half:(h + 1) * half].reshape(tm * ROWS, half)
        x = jnp.dot(eb[...], y, preferred_element_type=F32)
        n = x.shape[0] // 2
        parts.append((x[:n] + x[n:]) * factor[:, h * half:(h + 1) * half])
    mq = 2 * modes
    for j in range(tm):
        ssend[j] = jnp.concatenate([p[j * mq:(j + 1) * mq] for p in parts], 0).astype(BF16)

    def send_s(d, c):
        s_copy(lax.rem(me + d, tm)).start()
        return c

    lax.fori_loop(1, tm, send_s, 0)
    srecv[me] = ssend[me]

    def wait_s(d, c):
        s_from(lax.rem(me + tm - d, tm)).wait_recv()
        return c

    lax.fori_loop(1, tm, wait_s, 0)

    stacks = tm * share
    quarter = share // 2

    def unpack(s, c):
        x = srecv[s].astype(F32)
        zero = jnp.zeros((2 * mq, 128 - band), F32)
        for b in range(quarter):
            piece = jnp.concatenate([x[:, b * band:(b + 1) * band], zero], 1)
            for h in range(2):
                wf[pl.ds(s * share + h * quarter + b, mq, stride=stacks), :] = piece[h * mq:(h + 1) * mq]
        return c

    lax.fori_loop(0, tm, unpack, 0)
    for m in range(modes):
        s0 = wf[2 * m * stacks:(2 * m + 1) * stacks]
        s1 = wf[(2 * m + 1) * stacks:(2 * m + 2) * stacks]
        wmat[m, :stacks] = jnp.concatenate([s0, s1], 1).astype(BF16)
        wmat[m, stacks:] = jnp.concatenate([-s1, s0], 1).astype(BF16)

    sky_rows = beamb.shape[3]
    group = 8
    column = lax.broadcasted_iota(jnp.int32, (sky_rows, 256), 1) % 128
    rows_out = sky_rows // nf

    def one_mode(m, c):
        beam_copy(m).wait()

        def some(i, acc):
            x = beamb[m, pl.ds(i * group, group)]
            x = jnp.concatenate([x[:, 0], x[:, 1]], 2).reshape(group * sky_rows, 2 * stacks)
            z = jnp.dot(x, wmat[m], preferred_element_type=F32)
            for f in range(group):
                acc = jnp.where(column == i * group + f, z[f * sky_rows:(f + 1) * sky_rows], acc)
            return acc

        acc = lax.fori_loop(0, band // group, some, jnp.zeros((sky_rows, 256), F32))
        for j in range(nf):
            rows = acc[j * rows_out:(j + 1) * rows_out]
            skysend[m, j] = jnp.concatenate([rows[:, :128], rows[:, 128:]], 0).astype(BF16)

        def send_k(d, c):
            k_copy(m, lax.rem(mf + d, nf)).start()
            return c

        lax.fori_loop(1, nf, send_k, 0)
        skyrecv[m, mf] = skysend[m, mf]
        return c

    lax.fori_loop(0, modes, one_mode, 0)

    def filter_mode(m, c):
        def wait_k(d, c):
            k_from(m, lax.rem(mf + nf - d, nf)).wait_recv()
            return c

        lax.fori_loop(1, nf, wait_k, 0)
        rows = jnp.concatenate([skyrecv[m, s] for s in range(nf)], 1)
        out[m] = lax.dot_general(rows, klp[m], nt, preferred_element_type=F32).astype(BF16)
        return c

    lax.fori_loop(0, modes, filter_mode, 0)

    def drain_tm(d, c):
        j = lax.rem(me + d, tm)
        y_copy(j).wait_send()
        s_copy(j).wait_send()
        return c

    lax.fori_loop(1, tm, drain_tm, 0)

    def drain_f(d, c):
        j = lax.rem(mf + d, nf)
        for m in range(modes):
            k_copy(m, j).wait_send()
        return c

    lax.fori_loop(1, nf, drain_f, 0)


def local(visibilities, counts, beam_inverse, kl_modes):
    tm = lax.axis_size("tm")
    nf = lax.axis_size("freq")
    _, stacks, band, window = visibilities.shape
    modes, _, _, sky_rows, _ = beam_inverse.shape
    kept = kl_modes.shape[1]
    share = stacks // tm
    lanes = share * band
    g, e = factors(modes * tm, window, tm)
    any_space = pl.BlockSpec(memory_space=pl.ANY)
    rows_out = sky_rows // nf
    dma = pltpu.SemaphoreType.DMA
    filtered = pl.pallas_call(
        functools.partial(kernel, tm=tm, nf=nf, total=window * tm),
        out_shape=jax.ShapeDtypeStruct((modes, 2 * rows_out, kept), BF16),
        in_specs=[pl.BlockSpec(memory_space=pltpu.SMEM)] + [any_space] * 5,
        out_specs=pl.BlockSpec(memory_space=pltpu.VMEM),
        scratch_shapes=[
            pltpu.VMEM((tm, 2, lanes, window), BF16),
            pltpu.VMEM(beam_inverse.shape, BF16),
            pltpu.VMEM(kl_modes.shape, BF16),
            pltpu.VMEM((modes, kept, nf * 128), BF16),
            pltpu.VMEM(g.shape, BF16),
            pltpu.VMEM(e.shape, BF16),
            pltpu.VMEM((tm, ROWS, lanes), BF16),
            pltpu.VMEM((tm, ROWS, lanes), BF16),
            pltpu.VMEM((tm, 4 * modes, lanes // 2), BF16),
            pltpu.VMEM((tm, 4 * modes, lanes // 2), BF16),
            pltpu.VMEM((2 * modes * stacks, 128), F32),
            pltpu.VMEM((modes, 2 * stacks, 256), BF16),
            pltpu.VMEM((modes, nf, 2 * rows_out, 128), BF16),
            pltpu.VMEM((modes, nf, 2 * rows_out, 128), BF16),
            dma((tm,)), dma((modes,)), dma((3,)),
            dma((tm,)), dma((tm,)), dma((tm,)), dma((tm,)),
            dma((modes, nf)), dma((modes, nf)),
        ],
        compiler_params=pltpu.CompilerParams(
            collective_id=0, has_side_effects=True, vmem_limit_bytes=56 * 2**20),
    )(counts, visibilities.reshape(2, tm, lanes, window), beam_inverse, kl_modes, jnp.asarray(g), jnp.asarray(e))
    return filtered.reshape(modes, 2, rows_out, kept).transpose(2, 0, 1, 3)


def solution(mesh):
    in_specs = (
        P(None, None, "freq", "tm"),
        P(),
        P("tm", "freq", None, None, None),
        P("tm", None, None),
    )
    out_specs = P("freq", "tm", None, None)
    return jax.shard_map(local, mesh=mesh, in_specs=in_specs, out_specs=out_specs, check_vma=False)
```

time: 307 us -> 50.4 us (0.16)
  waiting for transfers between devices: 192 us -> 0 us
  Pallas kernels: 0 us -> 48.5 us
  local copies, waits for them, and re-layouts: 46.4 us -> 1.34 us
  blocking collectives: 28.6 us -> 0 us
  matrix products: 22.8 us -> 0 us
  other arithmetic: 8.51 us -> 0 us
  starting transfers between devices: 7.29 us -> 0 us
    all_to_all x1 -> x0, waiting for transfers between devices: 192 us -> none  [local(): lax.all_to_all(visibilities, 'tm', split_axis=1, concat_axis=3, tiled=True)]
    pallas_call x0 -> x1, Pallas kernels: none -> 48.5 us  [local(): pl.pallas_call(functools.partial(kernel, tm=tm, nf=nf, total=window * tm)...]
    all_to_all x7 -> x0, local copies, waits for them, and re-layouts: 34 us -> none  [the longest x2 33.6 us: local(): lax.all_to_all(visibilities, 'tm', split_axis=1, concat_axis=3, tiled=True)]
    all_to_all x2 -> x0, blocking collectives: 28.6 us -> none  [the longest x1 16.7 us: local(): lax.all_to_all(local_modes, 'tm', split_axis=0, concat_axis=2, tiled=True)]
    dot_general x3 -> x0, matrix products: 22.8 us -> none  [the longest x1 14.4 us: local(): jnp.einsum('mfplb,mqbf->mpqlf', beam_inverse, spectrum, preferred_element...]
    unnamed x5 -> x0, local copies, waits for them, and re-layouts: 10.9 us -> none
    another operation x4 -> x0, other arithmetic: 8.47 us -> none
    all_to_all x1 -> x0, starting transfers between devices: 7.29 us -> none  [local(): lax.all_to_all(visibilities, 'tm', split_axis=1, concat_axis=3, tiled=True)]
  transfers between devices with their start and end apart: 1 -> 0, of which waited for: 1 -> 0; matrix products, arithmetic and copies ran while one was open for 3% -> 0% of each run, Pallas kernels for 0% -> 0%
where the time goes in v1:
time: 50.4 us; the launch traced here: 49.8 us
  Pallas kernels  48.5 us (96%)
  local copies, waits for them, and re-layouts  1.34 us (3%)
    pallas_call x1, Pallas kernels, local(): pl.pallas_call(functools.partial(kernel, tm=tm, nf=nf, total=window * tm)...  48.5 us
    reshape x1, local copies, waits for them, and re-layouts, local(): return filtered.reshape(modes, 2, rows_out, kept).transpose(2, 0, 1, 3)  1.34 us

profile of v1, /device:TPU:0, one launch (start us, length us, event | category | flops | bytes accessed | tf_op | source)
XLA Modules:
  0.0 49.8 jit_solution(6775287259945001955)
XLA Ops:
  0.0 48.5 %shard_map.64 = bf16[4,16,128]{2,1,0:T(8,128)(2,1)} custom-call(s32[128]{0:T(128)} %counts.1, bf16[2,16,768,256]{3,2,1,0:T(8,128)(2,1)} %bitcast.5, bf16[4,96,2,64,128]{4,3,2,1,0:T(8,128)(2,1)} %beam.1, bf16[4,128,768]{2,1,0:T(8,128)(2,1)} %kl.1, bf16[48,512]{1,0:T(8,128)(2,1)} %constant.4.clone.g, bf16[256,512]{1,0:T(8,128)(2,1)} %constant.5.clone.e), custom_call_target="tpu_custom_call" | custom-call | tf_op jit(solution)/shard_map/pallas_call | solution.py:309
  48.5 1.3 %copy.9 = bf16[4,2,8,128]{3,1,0,2:T(2,128)(2,1)} copy(bf16[4,2,8,128]{3,2,1,0:T(8,128)(2,1)} %bitcast.6) | data formatting | bytes 32768 | tf_op jit(solution)/shard_map/reshape | solution.py:336

commit v2 on v1

--- a/solution.py
+++ b/solution.py
@@ -85,6 +85,23 @@
     g_copy = pltpu.make_async_copy(g, gb, misc_sem.at[0])
     e_copy = pltpu.make_async_copy(e, eb, misc_sem.at[1])
     kl_copy = pltpu.make_async_copy(kl, klb, misc_sem.at[2])
+    barrier = pltpu.get_barrier_semaphore()
+
+    per_x = tm // 4
+    offsets = [(dx, dr) for dr in range(per_x - 1, -1, -1) for dx in (2, 1, 3, 0) if (dx, dr) != (0, 0)]
+
+    def at(dx, dr):
+        x, r = me // per_x, me % per_x
+        y, c = r // 2, r % 2
+        y, c = lax.rem(y + dr // 2, 2), lax.rem(c + dr % 2, 2)
+        return lax.rem(x + dx, 4) * per_x + y * 2 + c
+
+    others = [at(dx, dr) for dx, dr in offsets]
+    bands = [lax.rem(mf + d, nf) for d in (4, 5, 3, 6, 2, 7, 1)]
+    for j in others:
+        pl.semaphore_signal(barrier, inc=1, device_id={"tm": j}, device_id_type=pl.DeviceIdType.MESH)
+    for j in bands:
+        pl.semaphore_signal(barrier, inc=1, device_id={"freq": j}, device_id_type=pl.DeviceIdType.MESH)
     g_copy.start()
 
     def vis_copy(j):
@@ -93,29 +110,11 @@
     def beam_copy(m):
         return pltpu.make_async_copy(beam.at[m], beamb.at[m], beam_sem.at[m])
 
-    def start_vis(d, c):
-        vis_copy(lax.rem(me + d, tm)).start()
-        return c
-
-    lax.fori_loop(1, tm + 1, start_vis, 0)
-    e_copy.start()
-    kl_copy.start()
-    for m in range(modes):
-        beam_copy(m).start()
-
-    barrier = pltpu.get_barrier_semaphore()
-
-    def greet_tm(d, c):
-        pl.semaphore_signal(barrier, inc=1, device_id={"tm": lax.rem(me + d, tm)}, device_id_type=pl.DeviceIdType.MESH)
-        return c
-
-    def greet_f(d, c):
-        pl.semaphore_signal(barrier, inc=1, device_id={"freq": lax.rem(mf + d, nf)}, device_id_type=pl.DeviceIdType.MESH)
-        return c
-
-    lax.fori_loop(1, tm, greet_tm, 0)
-    lax.fori_loop(1, nf, greet_f, 0)
-    pl.semaphore_wait(barrier, tm + nf - 2)
+    def start_vis(j, c):
+        vis_copy(j).start()
+        return c
+
+    lax.fori_loop(0, tm, start_vis, 0)
 
     def y_copy(j):
         return pltpu.make_async_remote_copy(
@@ -159,14 +158,20 @@
         low = strong - strong.astype(BF16).astype(F32)
         return jnp.concatenate([y, low], 0).astype(BF16)
 
-    def send_y(d, c):
-        j = lax.rem(me + d, tm)
-        ysend[j] = project(j)
+    def two(i, c):
+        for j in (2 * i, 2 * i + 1):
+            ysend[j] = project(j)
+        return c
+
+    lax.fori_loop(0, tm // 2, two, 0)
+    pl.semaphore_wait(barrier, tm + nf - 2)
+    for j in others:
         y_copy(j).start()
-        return c
-
-    lax.fori_loop(1, tm, send_y, 0)
-    yrecv[me] = project(me)
+    yrecv[me] = ysend[me]
+    e_copy.start()
+    kl_copy.start()
+    for m in range(modes):
+        beam_copy(m).start()
 
     kl_copy.wait()
 
@@ -186,12 +191,8 @@
     factor = jnp.sqrt(count) * (1.0 / math.sqrt(128.0 * total))
 
     e_copy.wait()
-
-    def wait_y(d, c):
-        y_from(lax.rem(me + tm - d, tm)).wait_recv()
-        return c
-
-    lax.fori_loop(1, tm, wait_y, 0)
+    for j in others:
+        y_from(j).wait_recv()
     parts = []
     for h in range(2):
         y = yrecv[:, :, h * half:(h + 1) * half].reshape(tm * ROWS, half)
@@ -202,18 +203,12 @@
     for j in range(tm):
         ssend[j] = jnp.concatenate([p[j * mq:(j + 1) * mq] for p in parts], 0).astype(BF16)
 
-    def send_s(d, c):
-        s_copy(lax.rem(me + d, tm)).start()
-        return c
-
-    lax.fori_loop(1, tm, send_s, 0)
+    for j in others:
+        s_copy(j).start()
     srecv[me] = ssend[me]
 
-    def wait_s(d, c):
-        s_from(lax.rem(me + tm - d, tm)).wait_recv()
-        return c
-
-    lax.fori_loop(1, tm, wait_s, 0)
+    for j in others:
+        s_from(j).wait_recv()
 
     stacks = tm * share
     quarter = share // 2
@@ -235,63 +230,44 @@
         wmat[m, stacks:] = jnp.concatenate([-s1, s0], 1).astype(BF16)
 
     sky_rows = beamb.shape[3]
-    group = 8
     column = lax.broadcasted_iota(jnp.int32, (sky_rows, 256), 1) % 128
     rows_out = sky_rows // nf
 
     def one_mode(m, c):
         beam_copy(m).wait()
 
-        def some(i, acc):
-            x = beamb[m, pl.ds(i * group, group)]
-            x = jnp.concatenate([x[:, 0], x[:, 1]], 2).reshape(group * sky_rows, 2 * stacks)
-            z = jnp.dot(x, wmat[m], preferred_element_type=F32)
-            for f in range(group):
-                acc = jnp.where(column == i * group + f, z[f * sky_rows:(f + 1) * sky_rows], acc)
-            return acc
-
-        acc = lax.fori_loop(0, band // group, some, jnp.zeros((sky_rows, 256), F32))
+        x = beamb[m]
+        x = jnp.concatenate([x[:, 0], x[:, 1]], 2).reshape(band * sky_rows, 2 * stacks)
+        z = jnp.dot(x, wmat[m], preferred_element_type=F32)
+        acc = jnp.zeros((sky_rows, 256), F32)
+        for f in range(band):
+            acc = jnp.where(column == f, z[f * sky_rows:(f + 1) * sky_rows], acc)
         for j in range(nf):
             rows = acc[j * rows_out:(j + 1) * rows_out]
             skysend[m, j] = jnp.concatenate([rows[:, :128], rows[:, 128:]], 0).astype(BF16)
 
-        def send_k(d, c):
-            k_copy(m, lax.rem(mf + d, nf)).start()
-            return c
-
-        lax.fori_loop(1, nf, send_k, 0)
+        for j in bands:
+            k_copy(m, j).start()
         skyrecv[m, mf] = skysend[m, mf]
         return c
 
     lax.fori_loop(0, modes, one_mode, 0)
 
     def filter_mode(m, c):
-        def wait_k(d, c):
-            k_from(m, lax.rem(mf + nf - d, nf)).wait_recv()
-            return c
-
-        lax.fori_loop(1, nf, wait_k, 0)
+        for j in bands:
+            k_from(m, j).wait_recv()
         rows = jnp.concatenate([skyrecv[m, s] for s in range(nf)], 1)
         out[m] = lax.dot_general(rows, klp[m], nt, preferred_element_type=F32).astype(BF16)
         return c
 
     lax.fori_loop(0, modes, filter_mode, 0)
 
-    def drain_tm(d, c):
-        j = lax.rem(me + d, tm)
+    for j in others:
         y_copy(j).wait_send()
         s_copy(j).wait_send()
-        return c
-
-    lax.fori_loop(1, tm, drain_tm, 0)
-
-    def drain_f(d, c):
-        j = lax.rem(mf + d, nf)
+    for j in bands:
         for m in range(modes):
             k_copy(m, j).wait_send()
-        return c
-
-    lax.fori_loop(1, nf, drain_f, 0)
 
 
 def local(visibilities, counts, beam_inverse, kl_modes):

time: 50.4 us -> 43.3 us (0.86)
  Pallas kernels: 48.5 us -> 41.8 us
    pallas_call x1, Pallas kernels: 48.5 us -> 41.8 us  [local(): pl.pallas_call(functools.partial(kernel, tm=tm, nf=nf, total=window * tm)...]
where the time goes in v2:
time: 43.3 us; the launch traced here: 43.1 us
  Pallas kernels  41.8 us (97%)
  local copies, waits for them, and re-layouts  1.34 us (3%)
    pallas_call x1, Pallas kernels, local(): pl.pallas_call(functools.partial(kernel, tm=tm, nf=nf, total=window * tm)...  41.8 us
    reshape x1, local copies, waits for them, and re-layouts, local(): return filtered.reshape(modes, 2, rows_out, kept).transpose(2, 0, 1, 3)  1.34 us

profile of v2, /device:TPU:0, one launch (start us, length us, event | category | flops | bytes accessed | tf_op | source)
XLA Modules:
  0.0 43.1 jit_solution(13567381708101045898)
XLA Ops:
  0.0 41.8 %shard_map.64 = bf16[4,16,128]{2,1,0:T(8,128)(2,1)} custom-call(s32[128]{0:T(128)} %counts.1, bf16[2,16,768,256]{3,2,1,0:T(8,128)(2,1)} %bitcast.5, bf16[4,96,2,64,128]{4,3,2,1,0:T(8,128)(2,1)} %beam.1, bf16[4,128,768]{2,1,0:T(8,128)(2,1)} %kl.1, bf16[48,512]{1,0:T(8,128)(2,1)} %constant.4.clone.g, bf16[256,512]{1,0:T(8,128)(2,1)} %constant.5.clone.e), custom_call_target="tpu_custom_call" | custom-call | tf_op jit(solution)/shard_map/pallas_call | solution.py:285
  41.8 1.3 %copy.9 = bf16[4,2,8,128]{3,1,0,2:T(2,128)(2,1)} copy(bf16[4,2,8,128]{3,2,1,0:T(8,128)(2,1)} %bitcast.6) | data formatting | bytes 32768 | tf_op jit(solution)/shard_map/reshape | solution.py:312

commit v3 on v2

--- a/solution.py
+++ b/solution.py
@@ -10,9 +10,14 @@
 from jax.experimental.pallas import tpu as pltpu
 from jax.sharding import PartitionSpec as P
 
-RANK = 12
-STRONG = (2, 3, 4, 5)
-ROWS = 2 * RANK + 2 * len(STRONG)
+RANK = 17
+STRONG = (7, 8, 9)
+DATA = 2 * RANK
+ROWS = DATA + 2 * len(STRONG)
+SUMS = 40
+AHEAD = 4
+GREETED = 4
+KNOWN = 3
 F32 = jnp.float32
 BF16 = jnp.bfloat16
 
@@ -49,11 +54,11 @@
 
 def factors(modes, window, windows):
     m, tc, step, expand, project = prolate(modes, window, windows)
-    order = list(STRONG) + [k for k in range(RANK) if k not in STRONG]
-    lead = len(STRONG)
-    rows = [(k, part) for part in (0, 1) for k in order[:lead]]
-    rows += [(k, part) for part in (0, 1) for k in order[lead:]]
-    g = np.zeros((2 * RANK, 2, window))
+    weak = [(k, part) for part in (0, 1) for k in range(RANK) if k not in STRONG]
+    strong = [(k, part) for part in (0, 1) for k in STRONG]
+    lead = DATA - 32
+    rows = weak[:lead] + strong + weak[lead:]
+    g = np.zeros((SUMS, 2, window))
     for at, (k, part) in enumerate(rows):
         re, im = project[k].real, project[k].imag
         g[at] = (re, -im) if part == 0 else (im, re)
@@ -64,14 +69,16 @@
             re, im = turned[:, k].real, turned[:, k].imag
             e[:, 0, w, at] = re if part == 0 else -im
             e[:, 1, w, at] = im if part == 0 else re
-    e[..., 2 * RANK:] = e[..., :2 * lead]
-    return halves(g.reshape(2 * RANK, 2 * window)), halves(e.reshape(2 * modes, windows * ROWS))
+    e[..., DATA:] = e[..., lead:lead + 2 * len(STRONG)]
+    g = g.reshape(SUMS, 2, 2, window // 2).transpose(2, 0, 1, 3)
+    g = np.stack([halves(core.reshape(SUMS, window)) for core in g])
+    return g, halves(e.reshape(2 * modes, windows * ROWS))
 
 
 def kernel(
-    counts, vis, beam, kl, g, e, out,
-    visb, beamb, klb, klp, gb, eb, ysend, yrecv, ssend, srecv, wf, wmat, skysend, skyrecv,
-    vis_sem, beam_sem, misc_sem, ys_sem, yr_sem, ss_sem, sr_sem, ks_sem, kr_sem,
+    countsh, vis, beam, kl, g, e, out,
+    counts, visb, beamb, klb, klp, gb, eb, pairsend, pairrecv, ysend, yrecv, ssend, srecv, wf, wmat, skysend, skyrecv,
+    vis_sem, beam_sem, misc_sem, ps_sem, pr_sem, x_sem, z_sem, ys_sem, yr_sem, ss_sem, sr_sem, ks_sem, kr_sem,
     *, tm, nf, total,
 ):
     me = lax.axis_index("tm")
@@ -82,26 +89,40 @@
     band = beamb.shape[1]
     window = visb.shape[3]
 
-    g_copy = pltpu.make_async_copy(g, gb, misc_sem.at[0])
+    core = me % 2
+    chip = me // 2
+    chips = tm // 2
+    g_copy = pltpu.make_async_copy(g.at[core], gb, misc_sem.at[0])
     e_copy = pltpu.make_async_copy(e, eb, misc_sem.at[1])
     kl_copy = pltpu.make_async_copy(kl, klb, misc_sem.at[2])
+    count_copy = pltpu.make_async_copy(countsh, counts, misc_sem.at[3])
     barrier = pltpu.get_barrier_semaphore()
 
-    per_x = tm // 4
-    offsets = [(dx, dr) for dr in range(per_x - 1, -1, -1) for dx in (2, 1, 3, 0) if (dx, dr) != (0, 0)]
-
-    def at(dx, dr):
-        x, r = me // per_x, me % per_x
-        y, c = r // 2, r % 2
-        y, c = lax.rem(y + dr // 2, 2), lax.rem(c + dr % 2, 2)
-        return lax.rem(x + dx, 4) * per_x + y * 2 + c
-
-    others = [at(dx, dr) for dx, dr in offsets]
-    bands = [lax.rem(mf + d, nf) for d in (4, 5, 3, 6, 2, 7, 1)]
-    for j in others:
-        pl.semaphore_signal(barrier, inc=1, device_id={"tm": j}, device_id_type=pl.DeviceIdType.MESH)
-    for j in bands:
-        pl.semaphore_signal(barrier, inc=1, device_id={"freq": j}, device_id_type=pl.DeviceIdType.MESH)
+    def at(dx, dy, dc):
+        x, y = chip // 2, chip % 2
+        return lax.rem(x + dx, chips // 2) * 4 + lax.rem(y + dy, 2) * 2 + lax.rem(core + dc, 2)
+
+    steps = [(dx, dy) for dy in (1, 0) for dx in (2, 1, 3, 0) if (dx, dy) != (0, 0)]
+    near = [(0, 1), (2, 0), (1, 0), (3, 0)]
+    far = [(2, 1), (1, 1), (3, 1)]
+    same = [at(dx, dy, 0) for dx, dy in far + near]
+    chip_order = [j // 2 for j in same] + [chip]
+    partner = at(0, 0, 1)
+    others = [at(dx, dy, dc) for dx, dy in steps for dc in (1, 0)] + [partner]
+    along_x = [at(dx, 0, 0) for dx in (2, 1, 3)]
+    across = at(0, 1, 0)
+    z, low_y = mf // 2, mf % 2
+    along_z = [lax.rem(z + dz, nf // 2) * 2 + low_y for dz in (2, 1, 3)]
+    beside = z * 2 + 1 - low_y
+    bands = [lax.rem(z + dz, nf // 2) * 2 + lax.rem(low_y + dy, 2) for dy in (1, 0) for dz in (2, 1, 3)] + [beside]
+
+    def signal(sem, **where):
+        pl.semaphore_signal(sem, inc=1, device_id=where, device_id_type=pl.DeviceIdType.MESH)
+
+    for j in along_x + [across, partner]:
+        signal(barrier, tm=j)
+    for j in along_z + [beside]:
+        signal(barrier, freq=j)
     g_copy.start()
 
     def vis_copy(j):
@@ -110,20 +131,26 @@
     def beam_copy(m):
         return pltpu.make_async_copy(beam.at[m], beamb.at[m], beam_sem.at[m])
 
-    def start_vis(j, c):
-        vis_copy(j).start()
-        return c
-
-    lax.fori_loop(0, tm, start_vis, 0)
-
-    def y_copy(j):
-        return pltpu.make_async_remote_copy(
-            src_ref=ysend.at[j], dst_ref=yrecv.at[me], send_sem=ys_sem.at[j], recv_sem=yr_sem.at[me],
-            device_id={"tm": j}, device_id_type=pl.DeviceIdType.MESH)
+    def chunk(k):
+        return 2 * chip_order[k % chips] + (1 - core if k < chips else core)
+
+    for k in range(AHEAD):
+        vis_copy(chunk(k)).start()
+    count_copy.start()
+
+    def pair_copy(i):
+        return pltpu.make_async_remote_copy(
+            src_ref=pairsend.at[i], dst_ref=pairrecv.at[i], send_sem=ps_sem.at[i], recv_sem=pr_sem.at[i],
+            device_id={"tm": partner}, device_id_type=pl.DeviceIdType.MESH)
+
+    def y_copy(k):
+        return pltpu.make_async_remote_copy(
+            src_ref=ysend.at[k], dst_ref=yrecv.at[chip], send_sem=ys_sem.at[k], recv_sem=yr_sem.at[chip],
+            device_id={"tm": same[k]}, device_id_type=pl.DeviceIdType.MESH)
 
     def y_from(s):
         return pltpu.make_async_remote_copy(
-            src_ref=ysend.at[s], dst_ref=yrecv.at[s], send_sem=ys_sem.at[s], recv_sem=yr_sem.at[s],
+            src_ref=ysend.at[s // 2], dst_ref=yrecv.at[s // 2], send_sem=ys_sem.at[s // 2], recv_sem=yr_sem.at[s // 2],
             device_id={"tm": s}, device_id_type=pl.DeviceIdType.MESH)
 
     def s_copy(j):
@@ -146,28 +173,53 @@
             src_ref=skysend.at[m, s], dst_ref=skyrecv.at[m, s], send_sem=ks_sem.at[m, s], recv_sem=kr_sem.at[m, s],
             device_id={"freq": s}, device_id_type=pl.DeviceIdType.MESH)
 
+    nt = (((1,), (1,)), ((), ()))
+
+    def project(k):
+        j = chunk(k)
+        vis_copy(j).wait()
+        if k + AHEAD < tm:
+            vis_copy(chunk(k + AHEAD)).start()
+        y = lax.dot_general(gb[:, :window], visb[j, 0], nt, preferred_element_type=F32)
+        y = y + lax.dot_general(gb[:, window:], visb[j, 1], nt, preferred_element_type=F32)
+        return y[:SUMS] + y[SUMS:]
+
     g_copy.wait()
-    nt = (((1,), (1,)), ((), ()))
-
-    def project(j):
-        vis_copy(j).wait()
-        y2 = lax.dot_general(gb[:, :window], visb[j, 0], nt, preferred_element_type=F32)
-        y2 = y2 + lax.dot_general(gb[:, window:], visb[j, 1], nt, preferred_element_type=F32)
-        y = y2[:2 * RANK] + y2[2 * RANK:]
-        strong = y[:2 * len(STRONG)]
-        low = strong - strong.astype(BF16).astype(F32)
-        return jnp.concatenate([y, low], 0).astype(BF16)
-
-    def two(i, c):
-        for j in (2 * i, 2 * i + 1):
-            ysend[j] = project(j)
-        return c
-
-    lax.fori_loop(0, tm // 2, two, 0)
-    pl.semaphore_wait(barrier, tm + nf - 2)
-    for j in others:
-        y_copy(j).start()
-    yrecv[me] = ysend[me]
+    for k in range(chips):
+        pairsend[k] = project(k)
+        if k == GREETED:
+            pl.semaphore_wait(barrier, 9)
+            for j in along_x:
+                signal(x_sem, tm=j)
+            for j in along_z:
+                signal(z_sem, freq=j)
+            for i in range(k):
+                pair_copy(i).start()
+        if k >= GREETED:
+            pair_copy(k).start()
+    row = lax.broadcasted_iota(jnp.int32, (ROWS - 32, lanes), 0) + 32
+
+    for k in range(chips):
+        own = project(k + chips)
+        pair_copy(k).wait_recv()
+        y = own + pairrecv[k]
+        low = y[:ROWS - 32]
+        low = low - low.astype(BF16).astype(F32)
+        tail = y[32:]
+        if ROWS > SUMS:
+            tail = jnp.concatenate([tail, tail[:ROWS - SUMS]], 0)
+        y = jnp.concatenate([y[:32], jnp.where(row < DATA, tail, low)], 0)
+        y = jnp.concatenate([y[:, :half], y[:, half:]], 0).astype(BF16)
+        if k < chips - 1:
+            ysend[k] = y
+        else:
+            yrecv[chip] = y
+        if k == KNOWN:
+            pl.semaphore_wait(x_sem, 3)
+            for i in range(k):
+                y_copy(i).start()
+        if KNOWN <= k < chips - 1:
+            y_copy(k).start()
     e_copy.start()
     kl_copy.start()
     for m in range(modes):
@@ -185,17 +237,18 @@
 
     lane = lax.broadcasted_iota(jnp.int32, (1, lanes), 1) // band
     share = lanes // band
+    count_copy.wait()
     count = jnp.zeros((1, lanes), F32)
     for i in range(share):
         count = jnp.where(lane == i, counts[me * share + i].astype(F32), count)
     factor = jnp.sqrt(count) * (1.0 / math.sqrt(128.0 * total))
 
     e_copy.wait()
-    for j in others:
+    for j in same:
         y_from(j).wait_recv()
     parts = []
     for h in range(2):
-        y = yrecv[:, :, h * half:(h + 1) * half].reshape(tm * ROWS, half)
+        y = yrecv[:, h * ROWS:(h + 1) * ROWS].reshape(chips * ROWS, half)
         x = jnp.dot(eb[...], y, preferred_element_type=F32)
         n = x.shape[0] // 2
         parts.append((x[:n] + x[n:]) * factor[:, h * half:(h + 1) * half])
@@ -228,6 +281,8 @@
         s1 = wf[(2 * m + 1) * stacks:(2 * m + 2) * stacks]
         wmat[m, :stacks] = jnp.concatenate([s0, s1], 1).astype(BF16)
         wmat[m, stacks:] = jnp.concatenate([-s1, s0], 1).astype(BF16)
+
+    pl.semaphore_wait(z_sem, 3)
 
     sky_rows = beamb.shape[3]
     column = lax.broadcasted_iota(jnp.int32, (sky_rows, 256), 1) % 128
@@ -262,8 +317,10 @@
 
     lax.fori_loop(0, modes, filter_mode, 0)
 
+    lax.fori_loop(0, chips, lambda i, c: (pair_copy(i).wait_send(), c)[1], 0)
+    for k in range(chips - 1):
+        y_copy(k).wait_send()
     for j in others:
-        y_copy(j).wait_send()
         s_copy(j).wait_send()
     for j in bands:
         for m in range(modes):
@@ -278,32 +335,36 @@
     kept = kl_modes.shape[1]
     share = stacks // tm
     lanes = share * band
-    g, e = factors(modes * tm, window, tm)
+    g, e = factors(modes * tm, 2 * window, tm // 2)
     any_space = pl.BlockSpec(memory_space=pl.ANY)
     rows_out = sky_rows // nf
     dma = pltpu.SemaphoreType.DMA
     filtered = pl.pallas_call(
         functools.partial(kernel, tm=tm, nf=nf, total=window * tm),
         out_shape=jax.ShapeDtypeStruct((modes, 2 * rows_out, kept), BF16),
-        in_specs=[pl.BlockSpec(memory_space=pltpu.SMEM)] + [any_space] * 5,
+        in_specs=[any_space] * 6,
         out_specs=pl.BlockSpec(memory_space=pltpu.VMEM),
         scratch_shapes=[
+            pltpu.SMEM(counts.shape, jnp.int32),
             pltpu.VMEM((tm, 2, lanes, window), BF16),
             pltpu.VMEM(beam_inverse.shape, BF16),
             pltpu.VMEM(kl_modes.shape, BF16),
             pltpu.VMEM((modes, kept, nf * 128), BF16),
-            pltpu.VMEM(g.shape, BF16),
+            pltpu.VMEM(g.shape[1:], BF16),
             pltpu.VMEM(e.shape, BF16),
-            pltpu.VMEM((tm, ROWS, lanes), BF16),
-            pltpu.VMEM((tm, ROWS, lanes), BF16),
+            pltpu.VMEM((tm // 2, SUMS, lanes), F32),
+            pltpu.VMEM((tm // 2, SUMS, lanes), F32),
+            pltpu.VMEM((tm // 2, 2 * ROWS, lanes // 2), BF16),
+            pltpu.VMEM((tm // 2, 2 * ROWS, lanes // 2), BF16),
             pltpu.VMEM((tm, 4 * modes, lanes // 2), BF16),
             pltpu.VMEM((tm, 4 * modes, lanes // 2), BF16),
             pltpu.VMEM((2 * modes * stacks, 128), F32),
             pltpu.VMEM((modes, 2 * stacks, 256), BF16),
             pltpu.VMEM((modes, nf, 2 * rows_out, 128), BF16),
             pltpu.VMEM((modes, nf, 2 * rows_out, 128), BF16),
-            dma((tm,)), dma((modes,)), dma((3,)),
-            dma((tm,)), dma((tm,)), dma((tm,)), dma((tm,)),
+            dma((tm,)), dma((modes,)), dma((4,)),
+            dma((tm // 2,)), dma((tm // 2,)), pltpu.SemaphoreType.REGULAR, pltpu.SemaphoreType.REGULAR,
+            dma((tm // 2,)), dma((tm // 2,)), dma((tm,)), dma((tm,)),
             dma((modes, nf)), dma((modes, nf)),
         ],
         compiler_params=pltpu.CompilerParams(

time: 43.3 us -> 37.9 us (0.88)
  Pallas kernels: 41.8 us -> 36.4 us
    pallas_call x1, Pallas kernels: 41.8 us -> 36.4 us  [local(): pl.pallas_call(functools.partial(kernel, tm=tm, nf=nf, total=window * tm)...]
where the time goes in v3:
time: 37.9 us; the launch traced here: 37.7 us
  Pallas kernels  36.4 us (96%)
  local copies, waits for them, and re-layouts  1.34 us (4%)
    pallas_call x1, Pallas kernels, local(): pl.pallas_call(functools.partial(kernel, tm=tm, nf=nf, total=window * tm)...  36.4 us
    reshape x1, local copies, waits for them, and re-layouts, local(): return filtered.reshape(modes, 2, rows_out, kept).transpose(2, 0, 1, 3)  1.34 us

profile of v3, /device:TPU:0, one launch (start us, length us, event | category | flops | bytes accessed | tf_op | source)
XLA Modules:
  0.0 37.7 jit_solution(13133266971714595480)
XLA Ops:
  0.0 36.4 %shard_map.64 = bf16[4,16,128]{2,1,0:T(8,128)(2,1)} custom-call(s32[128]{0:T(128)} %countsh.1, bf16[2,16,768,256]{3,2,1,0:T(8,128)(2,1)} %bitcast.5, bf16[4,96,2,64,128]{4,3,2,1,0:T(8,128)(2,1)} %beam.1, bf16[4,128,768]{2,1,0:T(8,128)(2,1)} %kl.1, bf16[2,80,512]{2,1,0:T(8,128)(2,1)} %constant.4.clone.g, bf16[256,320]{1,0:T(8,128)(2,1)} %constant.5.clone.e), custom_call_target="tpu_custom_call" | custom-call | tf_op jit(solution)/shard_map/pallas_call | solution.py:342
  36.4 1.3 %copy.9 = bf16[4,2,8,128]{3,1,0,2:T(2,128)(2,1)} copy(bf16[4,2,8,128]{3,2,1,0:T(8,128)(2,1)} %bitcast.6) | data formatting | bytes 32768 | tf_op jit(solution)/shard_map/reshape | solution.py:373

commit v4 on v3

--- a/solution.py
+++ b/solution.py
@@ -266,16 +266,18 @@
     stacks = tm * share
     quarter = share // 2
 
-    def unpack(s, c):
-        x = srecv[s].astype(F32)
-        zero = jnp.zeros((2 * mq, 128 - band), F32)
-        for b in range(quarter):
-            piece = jnp.concatenate([x[:, b * band:(b + 1) * band], zero], 1)
-            for h in range(2):
-                wf[pl.ds(s * share + h * quarter + b, mq, stride=stacks), :] = piece[h * mq:(h + 1) * mq]
+    zero = jnp.zeros((2 * mq, 128 - band), F32)
+    def unpack(i, c):
+        for s in range(4):
+            s = 4 * i + s
+            x = srecv[s].astype(F32)
+            for b in range(quarter):
+                piece = jnp.concatenate([x[:, b * band:(b + 1) * band], zero], 1)
+                for h in range(2):
+                    wf[pl.ds(s * share + h * quarter + b, mq, stride=stacks), :] = piece[h * mq:(h + 1) * mq]
         return c
 
-    lax.fori_loop(0, tm, unpack, 0)
+    lax.fori_loop(0, tm // 4, unpack, 0)
     for m in range(modes):
         s0 = wf[2 * m * stacks:(2 * m + 1) * stacks]
         s1 = wf[(2 * m + 1) * stacks:(2 * m + 2) * stacks]
@@ -290,7 +292,6 @@
 
     def one_mode(m, c):
         beam_copy(m).wait()
-
         x = beamb[m]
         x = jnp.concatenate([x[:, 0], x[:, 1]], 2).reshape(band * sky_rows, 2 * stacks)
         z = jnp.dot(x, wmat[m], preferred_element_type=F32)
@@ -308,14 +309,11 @@
 
     lax.fori_loop(0, modes, one_mode, 0)
 
-    def filter_mode(m, c):
+    for m in range(modes):
         for j in bands:
             k_from(m, j).wait_recv()
         rows = jnp.concatenate([skyrecv[m, s] for s in range(nf)], 1)
         out[m] = lax.dot_general(rows, klp[m], nt, preferred_element_type=F32).astype(BF16)
-        return c
-
-    lax.fori_loop(0, modes, filter_mode, 0)
 
     lax.fori_loop(0, chips, lambda i, c: (pair_copy(i).wait_send(), c)[1], 0)
     for k in range(chips - 1):

time: 37.9 us -> 37.1 us (0.979)
  Pallas kernels: 36.4 us -> 35.6 us
    pallas_call x1, Pallas kernels: 36.4 us -> 35.6 us  [local(): pl.pallas_call(functools.partial(kernel, tm=tm, nf=nf, total=window * tm)...]
where the time goes in v4:
time: 37.1 us; the launch traced here: 36.9 us
  Pallas kernels  35.6 us (96%)
  local copies, waits for them, and re-layouts  1.34 us (4%)
    pallas_call x1, Pallas kernels, local(): pl.pallas_call(functools.partial(kernel, tm=tm, nf=nf, total=window * tm)...  35.6 us
    reshape x1, local copies, waits for them, and re-layouts, local(): return filtered.reshape(modes, 2, rows_out, kept).transpose(2, 0, 1, 3)  1.34 us

profile of v4, /device:TPU:0, one launch (start us, length us, event | category | flops | bytes accessed | tf_op | source)
XLA Modules:
  0.0 36.9 jit_solution(18234518629699321)
XLA Ops:
  0.0 35.6 %shard_map.64 = bf16[4,16,128]{2,1,0:T(8,128)(2,1)} custom-call(s32[128]{0:T(128)} %countsh.1, bf16[2,16,768,256]{3,2,1,0:T(8,128)(2,1)} %bitcast.5, bf16[4,96,2,64,128]{4,3,2,1,0:T(8,128)(2,1)} %beam.1, bf16[4,128,768]{2,1,0:T(8,128)(2,1)} %kl.1, bf16[2,80,512]{2,1,0:T(8,128)(2,1)} %constant.4.clone.g, bf16[256,320]{1,0:T(8,128)(2,1)} %constant.5.clone.e), custom_call_target="tpu_custom_call" | custom-call | tf_op jit(solution)/shard_map/pallas_call | solution.py:340
  35.6 1.3 %copy.9 = bf16[4,2,8,128]{3,1,0,2:T(2,128)(2,1)} copy(bf16[4,2,8,128]{3,2,1,0:T(8,128)(2,1)} %bitcast.6) | data formatting | bytes 32768 | tf_op jit(solution)/shard_map/reshape | solution.py:371

commit v5 on v4

--- a/solution.py
+++ b/solution.py
@@ -15,9 +15,10 @@
 DATA = 2 * RANK
 ROWS = DATA + 2 * len(STRONG)
 SUMS = 40
+TOGETHER = 2
 AHEAD = 4
-GREETED = 4
-KNOWN = 3
+GREETED = 3
+KNOWN = 1
 F32 = jnp.float32
 BF16 = jnp.bfloat16
 
@@ -176,50 +177,58 @@
     nt = (((1,), (1,)), ((), ()))
 
     def project(k):
-        j = chunk(k)
-        vis_copy(j).wait()
-        if k + AHEAD < tm:
-            vis_copy(chunk(k + AHEAD)).start()
-        y = lax.dot_general(gb[:, :window], visb[j, 0], nt, preferred_element_type=F32)
-        y = y + lax.dot_general(gb[:, window:], visb[j, 1], nt, preferred_element_type=F32)
-        return y[:SUMS] + y[SUMS:]
+        js = [chunk(i) for i in range(k, k + TOGETHER)]
+        for j in js:
+            vis_copy(j).wait()
+        for i in range(k + AHEAD, min(k + AHEAD + TOGETHER, tm)):
+            vis_copy(chunk(i)).start()
+        y = 0.0
+        for p in (0, 1):
+            x = jnp.concatenate([visb[j, p] for j in js], 0)
+            y = y + lax.dot_general(gb[:, p * window:(p + 1) * window], x, nt, preferred_element_type=F32)
+        y = y[:SUMS] + y[SUMS:]
+        return [y[:, i * lanes:(i + 1) * lanes] for i in range(TOGETHER)]
 
     g_copy.wait()
-    for k in range(chips):
-        pairsend[k] = project(k)
-        if k == GREETED:
+    for k in range(0, chips, TOGETHER):
+        for i, y in enumerate(project(k)):
+            pairsend[k + i] = y
+        last = k + TOGETHER
+        if k <= GREETED < last:
             pl.semaphore_wait(barrier, 9)
             for j in along_x:
                 signal(x_sem, tm=j)
             for j in along_z:
                 signal(z_sem, freq=j)
-            for i in range(k):
+        if GREETED < last:
+            for i in range(0 if k <= GREETED else k, last):
                 pair_copy(i).start()
-        if k >= GREETED:
-            pair_copy(k).start()
     row = lax.broadcasted_iota(jnp.int32, (ROWS - 32, lanes), 0) + 32
 
-    for k in range(chips):
-        own = project(k + chips)
-        pair_copy(k).wait_recv()
+    def merge(k, own):
         y = own + pairrecv[k]
         low = y[:ROWS - 32]
         low = low - low.astype(BF16).astype(F32)
-        tail = y[32:]
-        if ROWS > SUMS:
-            tail = jnp.concatenate([tail, tail[:ROWS - SUMS]], 0)
-        y = jnp.concatenate([y[:32], jnp.where(row < DATA, tail, low)], 0)
+        y = jnp.concatenate([y[:32], jnp.where(row < DATA, y[32:], low)], 0)
         y = jnp.concatenate([y[:, :half], y[:, half:]], 0).astype(BF16)
         if k < chips - 1:
             ysend[k] = y
         else:
             yrecv[chip] = y
-        if k == KNOWN:
-            pl.semaphore_wait(x_sem, 3)
-            for i in range(k):
+
+    sent = 0
+    for k in range(0, chips, TOGETHER):
+        own = project(k + chips)
+        for i in range(TOGETHER):
+            pair_copy(k + i).wait_recv()
+        for i in range(TOGETHER):
+            merge(k + i, own[i])
+        if k + TOGETHER > KNOWN:
+            if not sent:
+                pl.semaphore_wait(x_sem, 3)
+            for i in range(sent, min(k + TOGETHER, chips - 1)):
                 y_copy(i).start()
-        if KNOWN <= k < chips - 1:
-            y_copy(k).start()
+            sent = k + TOGETHER
     e_copy.start()
     kl_copy.start()
     for m in range(modes):

time: 37.1 us -> 35.9 us (0.968)
  Pallas kernels: 35.6 us -> 34.4 us
    pallas_call x1, Pallas kernels: 35.6 us -> 34.4 us  [local(): pl.pallas_call(functools.partial(kernel, tm=tm, nf=nf, total=window * tm)...]
where the time goes in v5:
time: 35.9 us; the launch traced here: 35.7 us
  Pallas kernels  34.4 us (96%)
  local copies, waits for them, and re-layouts  1.34 us (4%)
    pallas_call x1, Pallas kernels, local(): pl.pallas_call(functools.partial(kernel, tm=tm, nf=nf, total=window * tm)...  34.4 us
    reshape x1, local copies, waits for them, and re-layouts, local(): return filtered.reshape(modes, 2, rows_out, kept).transpose(2, 0, 1, 3)  1.34 us

profile of v5, /device:TPU:0, one launch (start us, length us, event | category | flops | bytes accessed | tf_op | source)
XLA Modules:
  0.0 35.7 jit_solution(1886288509703221030)
XLA Ops:
  0.0 34.4 %shard_map.64 = bf16[4,16,128]{2,1,0:T(8,128)(2,1)} custom-call(s32[128]{0:T(128)} %countsh.1, bf16[2,16,768,256]{3,2,1,0:T(8,128)(2,1)} %bitcast.5, bf16[4,96,2,64,128]{4,3,2,1,0:T(8,128)(2,1)} %beam.1, bf16[4,128,768]{2,1,0:T(8,128)(2,1)} %kl.1, bf16[2,80,512]{2,1,0:T(8,128)(2,1)} %constant.4.clone.g, bf16[256,320]{1,0:T(8,128)(2,1)} %constant.5.clone.e), custom_call_target="tpu_custom_call" | custom-call | tf_op jit(solution)/shard_map/pallas_call | solution.py:349
  34.4 1.3 %copy.9 = bf16[4,2,8,128]{3,1,0,2:T(2,128)(2,1)} copy(bf16[4,2,8,128]{3,2,1,0:T(8,128)(2,1)} %bitcast.6) | data formatting | bytes 32768 | tf_op jit(solution)/shard_map/reshape | solution.py:380

commit v6 on v5

--- a/solution.py
+++ b/solution.py
@@ -16,7 +16,7 @@
 ROWS = DATA + 2 * len(STRONG)
 SUMS = 40
 TOGETHER = 2
-AHEAD = 4
+AHEAD = 6
 GREETED = 3
 KNOWN = 1
 F32 = jnp.float32
@@ -318,17 +318,18 @@
 
     lax.fori_loop(0, modes, one_mode, 0)
 
+    lax.fori_loop(0, chips, lambda i, c: (pair_copy(i).wait_send(), c)[1], 0)
+    for k in range(chips - 1):
+        y_copy(k).wait_send()
+    for j in others:
+        s_copy(j).wait_send()
+
     for m in range(modes):
         for j in bands:
             k_from(m, j).wait_recv()
         rows = jnp.concatenate([skyrecv[m, s] for s in range(nf)], 1)
         out[m] = lax.dot_general(rows, klp[m], nt, preferred_element_type=F32).astype(BF16)
 
-    lax.fori_loop(0, chips, lambda i, c: (pair_copy(i).wait_send(), c)[1], 0)
-    for k in range(chips - 1):
-        y_copy(k).wait_send()
-    for j in others:
-        s_copy(j).wait_send()
     for j in bands:
         for m in range(modes):
             k_copy(m, j).wait_send()

time: 35.9 us -> 35.7 us (level)
  no operation moved by 1% of the time
where the time goes in v6:
time: 35.7 us; the launch traced here: 35.6 us
  Pallas kernels  34.2 us (96%)
  local copies, waits for them, and re-layouts  1.34 us (4%)
    pallas_call x1, Pallas kernels, local(): pl.pallas_call(functools.partial(kernel, tm=tm, nf=nf, total=window * tm)...  34.2 us
    reshape x1, local copies, waits for them, and re-layouts, local(): return filtered.reshape(modes, 2, rows_out, kept).transpose(2, 0, 1, 3)  1.34 us

profile of v6, /device:TPU:0, one launch (start us, length us, event | category | flops | bytes accessed | tf_op | source)
XLA Modules:
  0.0 35.6 jit_solution(17658488078297066369)
XLA Ops:
  0.0 34.2 %shard_map.64 = bf16[4,16,128]{2,1,0:T(8,128)(2,1)} custom-call(s32[128]{0:T(128)} %countsh.1, bf16[2,16,768,256]{3,2,1,0:T(8,128)(2,1)} %bitcast.5, bf16[4,96,2,64,128]{4,3,2,1,0:T(8,128)(2,1)} %beam.1, bf16[4,128,768]{2,1,0:T(8,128)(2,1)} %kl.1, bf16[2,80,512]{2,1,0:T(8,128)(2,1)} %constant.4.clone.g, bf16[256,320]{1,0:T(8,128)(2,1)} %constant.5.clone.e), custom_call_target="tpu_custom_call" | custom-call | tf_op jit(solution)/shard_map/pallas_call | solution.py:350
  34.2 1.3 %copy.9 = bf16[4,2,8,128]{3,1,0,2:T(2,128)(2,1)} copy(bf16[4,2,8,128]{3,2,1,0:T(8,128)(2,1)} %bitcast.6) | data formatting | bytes 32768 | tf_op jit(solution)/shard_map/reshape | solution.py:381
